TPU v7x, 32 devices: a whole 2x2x4 slice. The times are simulated.
32 devices in a mesh: seq: 4 (over y, x), ctx: 2 (over core), head: 4 (over z).
Axes of the slice: x: 2, y: 2, z: 4, core: 2. Of those that a mesh axis runs over, the one named last changes fastest.
Arguments:
- queries: bfloat16 [4, 2, 512, 2048], P('seq', None, 'ctx', 'head'), may hold values from -8 to 8
- key_vectors: bfloat16 [4, 2, 512, 2048], P('seq', None, 'ctx', 'head'), may hold values from -8 to 8
- value_vectors: bfloat16 [4, 2, 512, 2048], P('seq', None, 'ctx', 'head'), may hold values from -6 to 6
- token_rates: float32 [4, 2, 512, 8], P('seq', None, 'ctx', 'head'), may hold values from 0.003 to 0.03
- fast_in: bfloat16 [8, 256, 512], P('head'), may hold values from -0.375 to 0.375
- fast_gate: bfloat16 [8, 256, 512], P('head'), may hold values from -0.375 to 0.375
- fast_out: bfloat16 [8, 512, 256], P('head'), may hold values from -0.25 to 0.25
- out_gain: float32 [2048], P('head'), may hold values from 0.1 to 1.9
- out_weight: bfloat16 [2048, 2048], P('head'), may hold values from -0.125 to 0.125
- cotangent: bfloat16 [4, 2, 512, 2048], P('seq', None, 'ctx', 'head'), may hold values from -6 to 6
Outputs:
- layer_out: bfloat16 [4, 2, 512, 2048], P('seq', None, 'ctx', 'head')
- weight_grad: float32 [2048, 2048], P('head', ('seq', 'ctx'))
- final_in: float32 [4, 8, 256, 512], P('seq', 'head')
- final_gate: float32 [4, 8, 256, 512], P('seq', 'head')
- final_out: float32 [4, 8, 512, 256], P('seq', 'head')
All inputs are finite; a program needn't handle non-finite values.
Results may differ from a plain program's by a relative error of at most 0.024.
Values may be sent and summed in bfloat16 or wider, within the bound.
A program may use at most 128 MiB of HBM per device.

v0:
```python
import math

import jax
import jax.numpy as jnp
from jax import lax
from jax.sharding import PartitionSpec as P


def passed_along(value, axis, steps):
    count = lax.axis_size(axis)
    pairs = [(source, (source + steps) % count) for source in range(count)]
    return lax.ppermute(value, axis, pairs)


def normalize_rms(values_in, epsilon):
    return values_in * lax.rsqrt(jnp.mean(values_in * values_in, axis=-1, keepdims=True) + epsilon)


def column_norms(weight):
    return jnp.sqrt(jnp.sum(weight * weight, axis=-2, keepdims=True) + 1e-06)


def renorm(weight, target):
    return weight * (target / jnp.sqrt(jnp.sum(weight * weight, axis=-2, keepdims=True) + 1e-06))


def shards(
    queries,
    key_vectors,
    value_vectors,
    token_rates,
    fast_in,
    fast_gate,
    fast_out,
    out_gain,
    out_weight,
    cotangent,
):
    local_heads, head_width, hidden_width = fast_in.shape
    block_count = queries.shape[1]
    row_count = queries.shape[2]
    ctx_index = lax.axis_index("ctx")
    query_rows = queries[0].reshape(block_count, row_count, local_heads, head_width)
    key_rows = key_vectors[0].reshape(block_count, row_count, local_heads, head_width)
    value_rows = value_vectors[0].reshape(block_count, row_count, local_heads, head_width)
    weight_in = fast_in.astype(jnp.float32)
    weight_gate = fast_gate.astype(jnp.float32)
    weight_out = fast_out.astype(jnp.float32)
    target_in = column_norms(weight_in)
    target_gate = column_norms(weight_gate)
    target_out = column_norms(weight_out)
    fast_outputs = []
    for block_index in range(block_count):
        query_norm = normalize_rms(query_rows[block_index].astype(jnp.float32), 1e-05).astype(
            jnp.bfloat16
        )
        key_norm = normalize_rms(key_rows[block_index].astype(jnp.float32), 1e-05).astype(
            jnp.bfloat16
        )
        round_in = weight_in.astype(jnp.bfloat16)
        round_gate = weight_gate.astype(jnp.bfloat16)
        round_out = weight_out.astype(jnp.bfloat16)
        hidden = (
            jax.nn.silu(
                jnp.einsum("thd,hdf->thf", query_norm, round_in, preferred_element_type=jnp.float32)
            )
            * jnp.einsum("thd,hdf->thf", query_norm, round_gate, preferred_element_type=jnp.float32)
        ).astype(jnp.bfloat16)
        fast_outputs.append(
            jnp.einsum("thf,hfd->thd", hidden, round_out, preferred_element_type=jnp.float32)
        )
        key_in = jnp.einsum("thd,hdf->thf", key_norm, round_in, preferred_element_type=jnp.float32)
        key_gate = jnp.einsum(
            "thd,hdf->thf", key_norm, round_gate, preferred_element_type=jnp.float32
        )
        sigmoid_in = jax.nn.sigmoid(key_in)
        active = key_in * sigmoid_in
        feature = (active * key_gate).astype(jnp.bfloat16)
        scaled_values = (
            token_rates[0, block_index][:, :, None] * value_rows[block_index].astype(jnp.float32)
        ).astype(jnp.bfloat16)
        d_feature = jnp.einsum(
            "thd,hfd->thf", scaled_values, round_out, preferred_element_type=jnp.float32
        )
        d_in = (d_feature * key_gate * sigmoid_in * (1.0 + key_in * (1.0 - sigmoid_in))).astype(
            jnp.bfloat16
        )
        d_gate = (d_feature * active).astype(jnp.bfloat16)
        update_in = jnp.einsum("thd,thf->hdf", key_norm, d_in, preferred_element_type=jnp.float32)
        update_gate = jnp.einsum(
            "thd,thf->hdf", key_norm, d_gate, preferred_element_type=jnp.float32
        )
        update_out = jnp.einsum(
            "thf,thd->hfd", feature, scaled_values, preferred_element_type=jnp.float32
        )
        total_in, total_gate, total_out = lax.psum((update_in, update_gate, update_out), "ctx")
        weight_in = renorm(weight_in + total_in, target_in)
        weight_gate = renorm(weight_gate + total_gate, target_gate)
        weight_out = renorm(weight_out + total_out, target_out)
    rim_keys, rim_values = passed_along((key_vectors[0], value_vectors[0]), "ctx", 1)
    earlier_keys = jnp.concatenate([jnp.zeros_like(rim_keys[:1]), rim_keys[:-1]], axis=0)
    earlier_values = jnp.concatenate([jnp.zeros_like(rim_values[:1]), rim_values[:-1]], axis=0)
    is_first = ctx_index == 0
    rim_keys = jnp.where(is_first, earlier_keys, rim_keys)
    rim_values = jnp.where(is_first, earlier_values, rim_values)
    window_keys = jnp.concatenate([rim_keys, key_vectors[0]], axis=1).reshape(
        block_count, 2 * row_count, local_heads, head_width
    )
    window_values = jnp.concatenate([rim_values, value_vectors[0]], axis=1).reshape(
        block_count, 2 * row_count, local_heads, head_width
    )
    scores = jnp.einsum(
        "cqhd,ckhd->chqk", query_rows, window_keys, preferred_element_type=jnp.float32
    ) * (1.0 / math.sqrt(head_width))
    query_pos = jnp.arange(row_count, dtype=jnp.int32)[:, None]
    key_pos = jnp.arange(2 * row_count, dtype=jnp.int32)[None, :]
    inside = (key_pos > query_pos) & (key_pos <= query_pos + row_count)
    block_ids = jnp.arange(block_count, dtype=jnp.int32)
    rim_open = (block_ids > 0) | (ctx_index != 0)
    allowed = inside[None, None] & (
        rim_open[:, None, None, None] | (key_pos >= row_count)[None, None]
    )
    scores = jnp.where(allowed, scores, -jnp.inf)
    largest = jnp.max(scores, axis=-1, keepdims=True)
    powers = jnp.exp(scores - largest)
    attn_weights = (powers / jnp.sum(powers, axis=-1, keepdims=True)).astype(jnp.bfloat16)
    attended = jnp.einsum(
        "chqk,ckhd->cqhd", attn_weights, window_values, preferred_element_type=jnp.float32
    )
    fast_stack = jnp.stack(fast_outputs)
    combined = (
        normalize_rms(fast_stack, 1e-05) * out_gain.reshape(local_heads, head_width) + attended
    ).astype(jnp.bfloat16)
    flat_rows = combined.reshape(block_count * row_count, local_heads * head_width)
    partial_out = jnp.dot(flat_rows, out_weight, preferred_element_type=jnp.float32)
    mixed_share = lax.psum_scatter(
        partial_out.astype(jnp.bfloat16), "head", scatter_dimension=1, tiled=True
    )
    layer_out = mixed_share.reshape(1, block_count, row_count, -1)
    piece = lax.all_gather(cotangent, "head", axis=3, tiled=True)
    grad_rows = jnp.einsum(
        "ti,tj->ij",
        flat_rows,
        piece.reshape(-1, piece.shape[3]),
        preferred_element_type=jnp.float32,
    )
    weight_grad = lax.psum_scatter(
        grad_rows.astype(jnp.bfloat16), ("seq", "ctx"), scatter_dimension=1, tiled=True
    ).astype(jnp.float32)
    return (layer_out, weight_grad, weight_in[None], weight_gate[None], weight_out[None])


def solution(mesh):
    return jax.shard_map(
        shards,
        mesh=mesh,
        in_specs=(
            P("seq", None, "ctx", "head"),
            P("seq", None, "ctx", "head"),
            P("seq", None, "ctx", "head"),
            P("seq", None, "ctx", "head"),
            P("head", None, None),
            P("head", None, None),
            P("head", None, None),
            P("head"),
            P("head", None),
            P("seq", None, "ctx", "head"),
        ),
        out_specs=(
            P("seq", None, "ctx", "head"),
            P("head", ("seq", "ctx")),
            P("seq", "head", None, None),
            P("seq", "head", None, None),
            P("seq", "head", None, None),
        ),
        check_vma=False,
    )
```

profile of v0, /device:TPU:0, one launch (start us, length us, event | category | flops | bytes accessed | tf_op | source)
XLA Modules:
  0.0 206.4 jit_solution(12462246118526753191)
XLA Ops:
  8.1 1.4 copy.147
  12.1 1.2 multiply_convert_fusion.15
  13.3 1.3 convolution_bitcast_fusion.7
  14.6 1.3 convolution_bitcast_fusion.8
  15.9 1.1 slice_convert_fusion
  17.0 2.2 %reshape.257 = f32[256,2,256]{2,1,0:T(2,128)} reshape(f32[1,1,256,512]{3,2,1,0:T(8,128)} %get-tuple-element.18) | data formatting | bytes 1048576 | tf_op jit(solution)/shard_map/convert_element_type | solution.py:80
  19.1 1.5 convolution_bitcast_fusion.6
  20.7 2.9 %fusion.37 = f32[2,512,256]{2,1,0:T(8,128)} fusion(f32[256,2,512]{2,0,1:T(8,128)S(1)} %copy-done.24, f32[256,2,512]{2,0,1:T(8,128)} %convolution_bitcast_fusion.8, f32[256,2,256]{2,1,0:T(2,128)S(1)} %copy-done.22, f32[256,2]{0,1:T(2,128)S(1)} %get-tuple-element.24), kind=kOutput, calls=%fused_computation.84 | convolution fusion | flops 136052736 | bytes 3672064 | tf_op jit(solution)/shard_map/thf,thd->hfd/dot_general | solution.py:93
  23.6 1.5 fusion.38
  25.1 1.6 fusion.47
  26.8 2.0 copy.164
  29.4 2.0 reshape_squeeze.2
  31.4 1.9 fusion.84
  33.2 1.1 copy.209
  34.3 1.0 copy.157
  35.4 1.2 copy.208
  37.7 2.1 %copy.169 = bf16[2,256,2,256]{3,1,2,0:T(8,128)(2,1)} copy(bf16[2,256,2,256]{1,3,2,0:T(8,128)(2,1)} %bitcast.117) | data formatting | bytes 1048576 | tf_op jit(solution)/shard_map/concatenate | solution.py:106
  40.1 2.5 %convolution_bitcast_fusion.10 = f32[256,2,512]{2,0,1:T(8,128)} fusion(bf16[2,256,512]{2,1,0:T(8,128)(2,1)S(1)} %copy-done.1, f32[256,2,256]{2,0,1:T(8,128)} %copy.145, f32[256,2]{0,1:T(2,128)S(1)} %add_rsqrt_fusion.4), kind=kOutput, calls=%fused_computation.20 | convolution fusion | flops 134479872 | bytes 2099200 | tf_op jit(solution)/shard_map/thd,hdf->thf/dot_general | solution.py:65
  42.6 3.1 %fusion.11 = f32[1,256,2,256]{1,3,2,0:T(8,128)} fusion(bf16[2,512,256]{2,1,0:T(8,128)(2,1)S(1)} %copy-done.8, bf16[2,256,512]{2,1,0:T(8,128)(2,1)} %param.15, f32[256,2,512]{2,0,1:T(8,128)} %convolution_bitcast_fusion.10, f32[256,2,256]{2,0,1:T(8,128)} %copy.145, f32[256,2]{0,1:T(2,128)S(1)} %add_rsqrt_fusion.4), kind=kOutput, calls=%fused_computation.33 | convolution fusion | flops 270270464 | bytes 3147776 | tf_op jit(solution)/shard_map/thf,hfd->thd/dot_general | solution.py:70
  45.7 1.0 slice.48
  47.6 2.1 %copy.168 = bf16[2,256,2,256]{3,1,2,0:T(8,128)(2,1)} copy(bf16[2,256,2,256]{1,3,2,0:T(8,128)(2,1)} %bitcast.126) | data formatting | bytes 1048576 | tf_op jit(solution)/shard_map/concatenate | solution.py:106
  49.6 3.6 %fusion.85 = (f32[2,2,256]{2,1,0:T(2,128)S(1)}, f32[2,2,256,512]{2,3,1,0:T(8,128)}) fusion(pred[2,256,512]{1,2,0:T(8,128)(4,1)S(1)} %broadcast_and_fusion, bf16[2,256,2,256]{3,2,1,0:T(2,128)(2,1)} %reshape_squeeze.2, bf16[2,256,2,256]{3,1,2,0:T(8,128)(2,1)} %copy.169, bf16[2,256,2,256]{3,1,2,0:T(8,128)(2,1)} %copy.168), kind=kOutput, calls=%fused_computation.148 | convolution fusion | flops 272630272 | bytes 3936256 | tf_op jit(solution)/shard_map/sub | solution.py:125
  53.2 1.0 slice.47
  55.1 1.6 fusion.12
  56.7 1.9 fusion.13
  60.7 1.3 convolution_bitcast_fusion.3
  62.9 3.2 %fusion.9 = f32[1,256,2,256]{1,3,2,0:T(8,128)} fusion(bf16[2,512,256]{2,1,0:T(8,128)(2,1)} %multiply_convert_fusion.8, bf16[2,256,512]{2,1,0:T(8,128)(2,1)} %multiply_convert_fusion.6, f32[256,2,512]{2,0,1:T(8,128)} %convolution_bitcast_fusion.3, f32[256,2,256]{2,0,1:T(8,128)} %copy.157, f32[256,2]{0,1:T(2,128)S(1)} %add_rsqrt_fusion.2), kind=kOutput, calls=%fused_computation.31 | convolution fusion | flops 270270464 | bytes 3147776 | tf_op jit(solution)/shard_map/thf,hfd->thd/dot_general | solution.py:70
  66.2 1.3 multiply_reduce_fusion.3
  67.5 3.4 %fusion.5 = bf16[2,256,2,256]{1,3,2,0:T(8,128)(2,1)} fusion(bf16[2,256,2,256]{1,3,2,0:T(8,128)(2,1)} %bitcast.130, bf16[2,256,2,256]{1,3,2,0:T(8,128)(2,1)} %bitcast.128, f32[2,2,256,512]{2,3,1,0:T(8,128)} %get-tuple-element.26, f32[2,2,256]{2,1,0:T(2,128)S(1)} %get-tuple-element.25, f32[1,256,2,256]{1,3,2,0:T(8,128)} %fusion.9, ...), kind=kOutput, calls=%fused_computation.27 | convolution fusion | flops 272891904 | bytes 4728832 | tf_op jit(solution)/shard_map/chqk,ckhd->cqhd/dot_general | solution.py:127
  70.9 2.0 copy.172
  72.9 1.9 copy.210
  74.8 2.9 %all-gather.2.cloned.1.call-done = bf16[1,2,256,2048]{3,2,1,0:T(8,128)(2,1)} async-done(((bf16[1,2,256,512]{3,2,1,0:T(8,128)(2,1)}), bf16[1,2,256,2048]{3,2,1,0:T(8,128)(2,1)}) %all-gather.2.cloned.1.call-update) | async-done | bytes 2097168 | tf_op jit(solution)/shard_map/all_gather | solution.py:140
  77.7 4.3 %convolution_convert_fusion = bf16[512,2048]{1,0:T(8,128)(2,1)} fusion(bf16[512,512]{1,0:T(8,128)(2,1)} %bitcast.131, bf16[512,2048]{1,0:T(8,128)(2,1)} %bitcast.133), kind=kOutput, calls=%fused_computation.1 | convolution fusion | flops 1074790400 | bytes 4718592 | tf_op jit(solution)/shard_map/ti,tj->ij/dot_general | solution.py:141
  83.9 2.2 %reshape.260 = f32[256,2,256]{2,1,0:T(2,128)} reshape(f32[1,1,256,512]{3,2,1,0:T(8,128)} %get-tuple-element.17) | data formatting | bytes 1048576 | tf_op jit(solution)/shard_map/convert_element_type | solution.py:80
  86.2 1.3 multiply_convert_fusion.13
  87.5 1.3 convolution_bitcast_fusion
  89.5 1.5 fusion.39
  91.0 1.6 fusion.40
  92.6 1.6 fusion.48
  94.3 3.7 %convolution_convert_fusion.1 = bf16[512,2048]{1,0:T(8,128)(2,1)} fusion(bf16[512,512]{1,0:T(8,128)(2,1)} %bitcast.132, bf16[512,2048]{1,0:T(8,128)(2,1)S(1)} %copy-done), kind=kOutput, calls=%fused_computation.2 | convolution fusion | flops 1074790400 | bytes 4718592 | tf_op jit(solution)/shard_map/dot_general | solution.py:135
  98.0 26.9 %reduce-scatter.5.cloned.1.call-done = bf16[512,256]{1,0:T(8,128)(2,1)} async-done(((bf16[512,2048]{1,0:T(8,128)(2,1)}), bf16[512,256]{1,0:T(8,128)(2,1)}) %reduce-scatter.5.cloned.1.call-update) | async-done | bytes 262160 | tf_op jit(solution)/shard_map/reduce_scatter | solution.py:147
  124.8 1.8 convert_element_type.157
  126.6 24.7 %all-reduce.7.cloned.1.call-done = (f32[2,256,512]{2,1,0:T(8,128)}, f32[2,256,512]{2,1,0:T(8,128)}, f32[2,512,256]{2,1,0:T(8,128)}) async-done(((f32[2,256,512]{2,1,0:T(8,128)}, f32[2,256,512]{2,1,0:T(8,128)}, f32[2,512,256]{2,1,0:T(8,128)}), (f32[2,256,512]{2,1,0:T(8,128)}, f32[2,256,512]{2,1,0:T(8,128)}, f32[2,512,256]{2,1,0:T(8,128)})) %all-reduce.7.cloned.1.call-update) | async-done | bytes 3145744 | tf_op jit(solution)/shard_map/psum | solution.py:96
  151.4 1.9 multiply_reduce_fusion
  155.3 1.2 multiply_bitcast_fusion
  156.4 1.3 multiply_bitcast_fusion.2
  157.7 1.3 multiply_bitcast_fusion.1
  159.0 40.3 %reduce-scatter.3.cloned.1.call-done = bf16[512,512]{1,0:T(8,128)(2,1)} async-done(((bf16[512,2048]{1,0:T(8,128)(2,1)}), bf16[512,512]{1,0:T(8,128)(2,1)}) %reduce-scatter.3.cloned.1.call-update) | async-done | bytes 524304 | tf_op jit(solution)/shard_map/reduce_scatter | solution.py:136
  (107 shorter events, 14.1 us)
Async XLA Ops:
  8.0 86.3 %copy-start = (bf16[512,2048]{1,0:T(8,128)(2,1)S(1)}, bf16[512,2048]{1,0:T(8,128)(2,1)}, u32[]{:S(2)}) copy-start(bf16[512,2048]{1,0:T(8,128)(2,1)} %param.18) | copy-start | bytes 6291460
  8.0 5.3 %copy-start.9 = (bf16[2,256,512]{2,1,0:T(8,128)(2,1)S(1)}, bf16[2,256,512]{2,1,0:T(8,128)(2,1)}, u32[]{:S(2)}) copy-start(bf16[2,256,512]{2,1,0:T(8,128)(2,1)} %param.15) | copy-start | bytes 1572868
  8.0 47.0 %all-reduce.9.cloned.1.call-start = ((), (), s32[]{:S(2)}) async-start(), calls=%async_computation.6 | async-start | bytes 6291456 | tf_op jit(solution)/shard_map/psum | solution.py:96
  9.5 0.8 copy-start.13
  11.0 3.5 %copy-start.1 = (bf16[2,256,512]{2,1,0:T(8,128)(2,1)S(1)}, bf16[2,256,512]{2,1,0:T(8,128)(2,1)}, u32[]{:S(2)}) copy-start(bf16[2,256,512]{2,1,0:T(8,128)(2,1)} %param.14) | copy-start | bytes 1572868
  12.1 3.8 %copy-start.19 = (bf16[1,2,256,512]{3,2,1,0:T(8,128)(2,1)S(1)}, bf16[1,2,256,512]{3,2,1,0:T(8,128)(2,1)}, u32[]{:S(2)}) copy-start(bf16[1,2,256,512]{3,2,1,0:T(8,128)(2,1)} %param.12) | copy-start | bytes 1572868
  14.6 4.5 %copy-start.26 = (f32[1,2,256,2]{2,3,1,0:T(2,128)S(1)}, f32[1,2,256,2]{2,3,1,0:T(2,128)}, u32[]{:S(2)}) copy-start(f32[1,2,256,2]{2,3,1,0:T(2,128)} %param.13) | copy-start | bytes 12292
  14.6 4.5 %copy-start.8 = (bf16[2,512,256]{2,1,0:T(8,128)(2,1)S(1)}, bf16[2,512,256]{2,1,0:T(8,128)(2,1)}, u32[]{:S(2)}) copy-start(bf16[2,512,256]{2,1,0:T(8,128)(2,1)} %param.16) | copy-start | bytes 1572868
  19.1 1.5 copy-start.22
  19.1 1.5 copy-start.24
  20.7 2.9 %copy-start.25 = (f32[256,2,512]{2,0,1:T(8,128)S(1)}, f32[256,2,512]{2,0,1:T(8,128)}, u32[]{:S(2)}) copy-start(f32[256,2,512]{2,0,1:T(8,128)} %convolution_bitcast_fusion.8) | copy-start | bytes 3145732
  26.7 51.0 %all-gather.2.cloned.1.call-start = ((), (), s32[]{:S(2)}) async-start(), calls=%async_computation.3 | async-start | bytes 2621440 | tf_op jit(solution)/shard_map/all_gather | solution.py:140
  28.8 24.4 %collective-permute-start = (bf16[2,256,512]{1,2,0:T(8,128)(2,1)}, bf16[2,256,512]{1,2,0:T(8,128)(2,1)}, u32[]{:S(2)}, u32[]{:S(2)}) collective-permute-start(bf16[2,256,512]{1,2,0:T(8,128)(2,1)} %bitcast.129), channel_id=1, source_target_pairs={{0,4},{4,0},{1,5},{5,1},{2,6},{6,2},{3,7},{7,3},{8,12},{12,8},{9,1... | collective-permute-start | bytes 1572872 | tf_op jit(solution)/shard_map/ppermute | solution.py:12
  29.3 16.5 %collective-permute-start.1 = (bf16[2,256,512]{1,2,0:T(8,128)(2,1)}, bf16[2,256,512]{1,2,0:T(8,128)(2,1)}, u32[]{:S(2)}, u32[]{:S(2)}) collective-permute-start(bf16[2,256,512]{1,2,0:T(8,128)(2,1)} %bitcast.116), channel_id=1, source_target_pairs={{0,4},{4,0},{1,5},{5,1},{2,6},{6,2},{3,7},{7,3},{8,12},{12,8},{9,1... | collective-permute-start | bytes 1572872 | tf_op jit(solution)/shard_map/ppermute | solution.py:12
  29.3 95.5 %reduce-scatter.5.cloned.1.call-start = ((), (), s32[]{:S(2)}) async-start(), calls=%async_computation.4 | async-start | bytes 2359296 | tf_op jit(solution)/shard_map/reduce_scatter | solution.py:147
  33.2 6.6 %copy-start.27 = (f32[512]{0:T(512)S(1)}, f32[512]{0:T(512)}, u32[]{:S(2)}) copy-start(f32[512]{0:T(512)} %param.17) | copy-start | bytes 6148
  55.1 1.6 copy-start.2
  55.1 3.6 %copy-start.6 = (f32[2,512,256]{2,1,0:T(8,128)S(1)}, f32[2,512,256]{2,1,0:T(8,128)}, u32[]{:S(2)}) copy-start(f32[2,512,256]{2,1,0:T(8,128)} %get-tuple-element.14) | copy-start | bytes 3145732
  56.7 2.9 %copy-start.4 = (f32[2,256,512]{2,1,0:T(8,128)S(1)}, f32[2,256,512]{2,1,0:T(8,128)}, u32[]{:S(2)}) copy-start(f32[2,256,512]{2,1,0:T(8,128)} %get-tuple-element.16) | copy-start | bytes 3145732
  58.7 2.0 copy-start.20
  59.6 2.3 %copy-start.10 = (bf16[2,256,512]{2,1,0:T(8,128)(2,1)S(1)}, bf16[2,256,512]{2,1,0:T(8,128)(2,1)}, u32[]{:S(2)}) copy-start(bf16[2,256,512]{2,1,0:T(8,128)(2,1)} %param.15) | copy-start | bytes 1572868
  59.8 0.8 copy-start.12
  82.1 0.9 copy-start.17
  82.1 69.3 %all-reduce.7.cloned.1.call-start = ((), (), s32[]{:S(2)}) async-start(), calls=%async_computation.5 | async-start | bytes 6291456 | tf_op jit(solution)/shard_map/psum | solution.py:96
  86.1 2.7 %copy-start.23 = (bf16[2,256,512]{2,1,0:T(8,128)(2,1)S(1)}, bf16[2,256,512]{2,1,0:T(8,128)(2,1)}, u32[]{:S(2)}) copy-start(bf16[2,256,512]{2,1,0:T(8,128)(2,1)} %multiply_convert_fusion.6) | copy-start | bytes 1572868
  86.2 3.0 %copy-start.18 = (bf16[2,512,256]{2,1,0:T(8,128)(2,1)S(1)}, bf16[2,512,256]{2,1,0:T(8,128)(2,1)}, u32[]{:S(2)}) copy-start(bf16[2,512,256]{2,1,0:T(8,128)(2,1)} %multiply_convert_fusion.8) | copy-start | bytes 1572868
  86.2 3.0 %copy-start.21 = (f32[256,2,256]{2,1,0:T(2,128)S(1)}, f32[256,2,256]{2,1,0:T(2,128)}, u32[]{:S(2)}) copy-start(f32[256,2,256]{2,1,0:T(2,128)} %reshape.260) | copy-start | bytes 1572868
  94.2 105.0 %reduce-scatter.3.cloned.1.call-start = ((), (), s32[]{:S(2)}) async-start(), calls=%async_computation.2 | async-start | bytes 2621440 | tf_op jit(solution)/shard_map/reduce_scatter | solution.py:136
  151.4 1.9 copy-start.5
  151.4 2.2 %copy-start.15 = (f32[2,256,512]{2,1,0:T(8,128)S(1)}, f32[2,256,512]{2,1,0:T(8,128)}, u32[]{:S(2)}) copy-start(f32[2,256,512]{2,1,0:T(8,128)} %get-tuple-element.11) | copy-start | bytes 3145732
  151.4 2.5 %copy-start.3 = (f32[2,256,512]{2,1,0:T(8,128)S(1)}, f32[2,256,512]{2,1,0:T(8,128)}, u32[]{:S(2)}) copy-start(f32[2,256,512]{2,1,0:T(8,128)} %get-tuple-element.15) | copy-start | bytes 3145732
  151.4 2.6 %copy-start.11 = (bf16[2,256,512]{2,1,0:T(8,128)(2,1)S(1)}, bf16[2,256,512]{2,1,0:T(8,128)(2,1)}, u32[]{:S(2)}) copy-start(bf16[2,256,512]{2,1,0:T(8,128)(2,1)} %param.15) | copy-start | bytes 1572868
  151.4 3.0 %copy-start.14 = (f32[2,256,512]{2,1,0:T(8,128)S(1)}, f32[2,256,512]{2,1,0:T(8,128)}, u32[]{:S(2)}) copy-start(f32[2,256,512]{2,1,0:T(8,128)} %get-tuple-element.12) | copy-start | bytes 3145732
  153.5 1.4 copy-start.7
  153.5 1.7 copy-start.16
Sparse Core Ops, SparseCore 0:
  26.8 26.0 all-reduce.8
  82.2 42.5 reduce-scatter.4
  127.9 23.3 all-reduce.6
  154.2 45.0 reduce-scatter.2
Sparse Core Ops, SparseCore 1:
  29.4 48.2 all-gather.1
where the time goes:
time: 208 us; the launch traced here: 206 us
  waiting for transfers between devices  94.9 us (46%)
  matrix products  41.8 us (20%)
  local copies, waits for them, and re-layouts  32.1 us (15%)
  other arithmetic  21.1 us (10%)
  between operations  15.6 us (8%)
    reduce_scatter x1, waiting for transfers between devices, shards(): lax.psum_scatter(partial_out.astype(jnp.bfloat16), 'head', scatter_dimens...  40.3 us
    reduce_scatter x1, waiting for transfers between devices, shards(): lax.psum_scatter(grad_rows.astype(jnp.bfloat16), ('seq', 'ctx'), scatter_...  26.9 us
    psum x2, waiting for transfers between devices, shards(): lax.psum((update_in, update_gate, update_out), 'ctx')  24.7 us
    unnamed x61, local copies, waits for them, and re-layouts  11.3 us
    dot_general x2, matrix products, shards(): jnp.einsum('thf,hfd->thd', hidden, round_out, preferred_element_type=jnp....  6.37 us
    dot_general x2, matrix products, shards(): jnp.einsum('thf,thd->hfd', feature, scaled_values, preferred_element_type...  4.43 us
    dot_general x1, matrix products, shards(): jnp.einsum('ti,tj->ij', flat_rows, piece.reshape(-1, piece.shape[3]), pre...  4.34 us
    convert_element_type x2, local copies, waits for them, and re-layouts, shards(): value_rows[block_index].astype(jnp.float32)  4.32 us
  transfers between devices with their start and end apart: 7, of which 4 were waited for; matrix products, arithmetic and copies ran while one was open for 34% of the time, Pallas kernels for 0%

commit v1 on v0

--- a/solution.py
+++ b/solution.py
@@ -1,8 +1,11 @@
+import functools
 import math
 
 import jax
 import jax.numpy as jnp
 from jax import lax
+from jax.experimental import pallas as pl
+from jax.experimental.pallas import tpu as pltpu
 from jax.sharding import PartitionSpec as P
 
 
@@ -149,10 +152,568 @@
     ).astype(jnp.float32)
     return (layer_out, weight_grad, weight_in[None], weight_gate[None], weight_out[None])
 
+BF = jnp.bfloat16
+F32 = jnp.float32
+
+
+def mm(left, right):
+    return jnp.dot(left, right, preferred_element_type=F32)
+
+
+def mm_tn(left, right):
+    return lax.dot_general(left, right, (((0,), (0,)), ((), ())), preferred_element_type=F32)
+
+
+def mm_nt(left, right):
+    return lax.dot_general(left, right, (((1,), (1,)), ((), ())), preferred_element_type=F32)
+
+
+def layer_kernel(
+    seqs,
+    heads,
+    q_ref,
+    k_ref,
+    v_ref,
+    rate_ref,
+    win_ref,
+    wgate_ref,
+    wout_ref,
+    gain_ref,
+    ow_ref,
+    cot_ref,
+    out_ref,
+    grad_ref,
+    fin_ref,
+    fgate_ref,
+    fout_ref,
+    qh,
+    kh,
+    vh,
+    svh,
+    sv_all,
+    cot_all,
+    rin,
+    rgate,
+    rout,
+    acc_in,
+    acc_gate,
+    acc_out,
+    fast,
+    comb,
+    comb_t,
+    own,
+    part,
+    up_buf,
+    down_buf,
+    gsend,
+    grecv,
+    core_s,
+    core_r,
+    cot_core_s,
+    cot_core_r,
+    ag_up_s,
+    ag_down_s,
+    ag_r,
+    comb_s,
+    comb_r,
+    fin_s,
+    fin_r,
+    up_s,
+    up_r,
+    down_s,
+    down_r,
+    g_s,
+    g_r,
+    local_s,
+):
+    s = lax.axis_index("seq")
+    c = lax.axis_index("ctx")
+    h = lax.axis_index("head")
+    o = 1 - c
+    blocks, rows = q_ref.shape[1], q_ref.shape[2]
+    dh = win_ref.shape[1]
+    mine = pl.ds(pl.multiple_of(c * dh, dh), dh)
+    theirs = pl.ds(pl.multiple_of(o * dh, dh), dh)
+    last = heads - 1
+
+    def remote(src, dst, send, recv, where):
+        return pltpu.make_async_remote_copy(
+            src_ref=src,
+            dst_ref=dst,
+            send_sem=send,
+            recv_sem=recv,
+            device_id=where,
+            device_id_type=pl.DeviceIdType.MESH,
+        )
+
+    barrier = pltpu.get_barrier_semaphore()
+    for s2 in range(seqs):
+        for c2 in range(2):
+
+            @pl.when((s2 != s) | (c2 != c))
+            def _():
+                pl.semaphore_signal(
+                    barrier,
+                    inc=1,
+                    device_id={"seq": s2, "ctx": c2},
+                    device_id_type=pl.DeviceIdType.MESH,
+                )
+
+    @pl.when(h < last)
+    def _():
+        pl.semaphore_signal(
+            barrier, inc=1, device_id={"head": h + 1}, device_id_type=pl.DeviceIdType.MESH
+        )
+
+    @pl.when(h > 0)
+    def _():
+        pl.semaphore_signal(
+            barrier, inc=1, device_id={"head": h - 1}, device_id_type=pl.DeviceIdType.MESH
+        )
+
+    ends = (h == 0).astype(jnp.int32) + (h == last).astype(jnp.int32)
+    pl.semaphore_wait(barrier, 2 * seqs - 1 + 2 - ends)
+
+    def cot_up(owner, src):
+        return remote(
+            src, cot_all.at[owner, :, c], ag_up_s.at[owner], ag_r.at[owner], {"head": h + 1}
+        )
+
+    def cot_down(owner, src):
+        return remote(
+            src, cot_all.at[owner, :, c], ag_down_s.at[owner], ag_r.at[owner], {"head": h - 1}
+        )
+
+    def cot_core(owner, src):
+        return remote(
+            src, cot_all.at[owner, :, c], cot_core_s.at[owner], cot_core_r.at[owner], {"ctx": o}
+        )
+
+    def exchange(index, src, dst):
+        return remote(src, dst, core_s.at[index], core_r.at[index], {"ctx": o})
+
+    swaps = [
+        exchange(0, k_ref.at[0, :, :, theirs], kh.at[:, c]),
+        exchange(1, sv_all.at[:, :, theirs], svh.at[:, c]),
+        exchange(2, q_ref.at[0, :, :, theirs], qh.at[:, c]),
+        exchange(3, v_ref.at[0, :, :, theirs], vh.at[:, c]),
+    ]
+    swaps[0].start()
+    swaps[2].start()
+    swaps[3].start()
+
+    @pl.when(h < last)
+    def _():
+        cot_up(h, cot_ref.at[0]).start()
+
+    @pl.when(h > 0)
+    def _():
+        cot_down(h, cot_ref.at[0]).start()
+
+    for b in range(blocks):
+        for i in range(2):
+            cols = slice(i * dh, (i + 1) * dh)
+            rate = rate_ref[0, b, :, i : i + 1]
+            sv_all[b, :, cols] = (rate * v_ref[0, b, :, cols].astype(F32)).astype(BF)
+    swaps[1].start()
+    cot_core(h, cot_ref.at[0]).start()
+    locals_ = [
+        pltpu.make_async_copy(k_ref.at[0, :, :, mine], kh.at[:, c], local_s.at[0]),
+        pltpu.make_async_copy(sv_all.at[:, :, mine], svh.at[:, c], local_s.at[1]),
+        pltpu.make_async_copy(q_ref.at[0, :, :, mine], qh.at[:, c], local_s.at[2]),
+        pltpu.make_async_copy(v_ref.at[0, :, :, mine], vh.at[:, c], local_s.at[3]),
+        pltpu.make_async_copy(cot_ref.at[0], cot_all.at[h, :, c], local_s.at[4]),
+    ]
+    for copy in locals_:
+        copy.start()
+
+    def squares(weight):
+        return jnp.sum(weight * weight, axis=0, keepdims=True) + 1e-06
+
+    targets = []
+    for src, kept in ((win_ref, rin), (wgate_ref, rgate), (wout_ref, rout)):
+        kept[...] = src[c]
+        targets.append(jnp.sqrt(squares(src[c].astype(F32))))
+    for copy in locals_:
+        copy.wait()
+    for copy in swaps:
+        copy.wait()
+
+    def fast_block(b):
+        @pl.loop(0, 2)
+        def _(i):
+            key_norm = normalize_rms(kh[b, i].astype(F32), 1e-05).astype(BF)
+            key_in = mm(key_norm, rin[...])
+            key_gate = mm(key_norm, rgate[...])
+            scaled = svh[b, i]
+            d_feature = mm_nt(scaled, rout[...])
+            sigma = jax.nn.sigmoid(key_in)
+            active = key_in * sigma
+            feature = (active * key_gate).astype(BF)
+            d_in = (d_feature * key_gate * sigma * (1.0 + key_in * (1.0 - sigma))).astype(BF)
+            d_gate = (d_feature * active).astype(BF)
+            up_in = mm_tn(key_norm, d_in)
+            up_gate = mm_tn(key_norm, d_gate)
+            up_out = mm_tn(feature, scaled)
+
+            @pl.when(i == 0)
+            def _():
+                acc_in[...] = up_in
+                acc_gate[...] = up_gate
+                acc_out[...] = up_out
+
+            @pl.when(i == 1)
+            def _():
+                acc_in[...] += up_in
+                acc_gate[...] += up_gate
+                acc_out[...] += up_out
+
+            query_norm = normalize_rms(qh[b, i].astype(F32), 1e-05).astype(BF)
+            first = mm(query_norm, rin[...])
+            hidden = (first * jax.nn.sigmoid(first) * mm(query_norm, rgate[...])).astype(BF)
+            fast[i] = mm(hidden, rout[...])
+
+        for kept, acc, final, target, start in (
+            (rin, acc_in, fin_ref, targets[0], win_ref),
+            (rgate, acc_gate, fgate_ref, targets[1], wgate_ref),
+            (rout, acc_out, fout_ref, targets[2], wout_ref),
+        ):
+            weight = (start[c].astype(F32) if b == 0 else final[0, c]) + acc[...]
+            weight = weight * (target / jnp.sqrt(squares(weight)))
+            final[0, c] = weight
+            kept[...] = weight.astype(BF)
+
+    row = lax.broadcasted_iota(jnp.int32, (rows, rows), 0)
+    col = lax.broadcasted_iota(jnp.int32, (rows, rows), 1)
+    scale = 1.0 / math.sqrt(dh)
+
+    def attend(b, i):
+        query = qh[b, i]
+        now = jnp.where(col <= row, mm_nt(query, kh[b, i]) * scale, -jnp.inf)
+        largest = jnp.max(now, axis=-1, keepdims=True)
+        if b == 0 and i == 0:
+            powers = jnp.exp(now - largest)
+            total = jnp.sum(powers, axis=-1, keepdims=True)
+            return mm((powers / total).astype(BF), vh[b, i])
+        before = (b, 0) if i == 1 else (b - 1, 1)
+        old = jnp.where(col > row, mm_nt(query, kh[before]) * scale, -jnp.inf)
+        largest = jnp.maximum(largest, jnp.max(old, axis=-1, keepdims=True))
+        powers = jnp.exp(now - largest)
+        old_powers = jnp.exp(old - largest)
+        total = jnp.sum(powers, axis=-1, keepdims=True) + jnp.sum(
+            old_powers, axis=-1, keepdims=True
+        )
+        return mm((powers / total).astype(BF), vh[b, i]) + mm(
+            (old_powers / total).astype(BF), vh[before]
+        )
+
+    def comb_copy(b):
+        return remote(
+            comb.at[b, o], own.at[b, :, mine], comb_s.at[b], comb_r.at[b], {"ctx": o}
+        )
+
+    def combine(b):
+        for i in range(2):
+            value = (
+                normalize_rms(fast[i], 1e-05) * gain_ref[pl.ds(c, 1), :] + attend(b, i)
+            ).astype(BF)
+            comb[b, i] = value
+            at = (b * 2 + i) * rows
+            comb_t[:, at : at + rows] = value.T
+        comb_copy(b).start()
+        own[b, :, mine] = comb[b, c]
+
+    width = ow_ref.shape[1] // heads
+
+    def up_copy(b, d):
+        return remote(
+            part.at[b, d], up_buf.at[b, d], up_s.at[b, d], up_r.at[b, d], {"head": h + 1}
+        )
+
+    def down_copy(b, d):
+        return remote(
+            part.at[b, d], down_buf.at[b, d], down_s.at[b, d], down_r.at[b, d], {"head": h - 1}
+        )
+
+    def project(b):
+        comb_copy(b).wait()
+        rows_in = own[b]
+        for d in range(heads):
+            part[b, d] = mm(rows_in, ow_ref[:, d * width : (d + 1) * width]).astype(BF)
+
+        @pl.when(h == 0)
+        def _():
+            for d in range(last, 0, -1):
+                up_copy(b, d).start()
+
+        @pl.when(h == last)
+        def _():
+            for d in range(last):
+                down_copy(b, d).start()
+
+    def add(b, d, buf):
+        part[b, d] = (part[b, d].astype(F32) + buf[b, d].astype(F32)).astype(BF)
+
+    def forward(b):
+        for step in range(heads - 2):
+            d = last - step
+
+            @pl.when((h > 0) & (h < d))
+            def _(d=d):
+                up_copy(b, d).wait_recv()
+                add(b, d, up_buf)
+                up_copy(b, d).start()
+
+            e = step
+
+            @pl.when((h < last) & (h > e))
+            def _(e=e):
+                down_copy(b, e).wait_recv()
+                add(b, e, down_buf)
+                down_copy(b, e).start()
+
+    def finish(b):
+        @pl.when(h > 0)
+        def _():
+            up_copy(b, h).wait_recv()
+            add(b, h, up_buf)
+
+        @pl.when(h < last)
+        def _():
+            down_copy(b, h).wait_recv()
+            add(b, h, down_buf)
+
+        out_ref[0, b] = part[b, h]
+        for d in range(heads):
+
+            @pl.when(d > h)
+            def _(d=d):
+                up_copy(b, d).wait_send()
+
+            @pl.when(d < h)
+            def _(d=d):
+                down_copy(b, d).wait_send()
+
+    def gather_step(t):
+        @pl.when(h - t >= 0)
+        def _():
+            owner = h - t
+            piece = cot_all.at[owner, :, c]
+            cot_up(owner, piece).wait_recv()
+            cot_core(owner, piece).start()
+
+            @pl.when(h < last)
+            def _():
+                cot_up(owner, piece).start()
+
+        @pl.when(h + t <= last)
+        def _():
+            owner = h + t
+            piece = cot_all.at[owner, :, c]
+            cot_down(owner, piece).wait_recv()
+            cot_core(owner, piece).start()
+
+            @pl.when(h > 0)
+            def _():
+                cot_down(owner, piece).start()
+
+    def g_copy(j, c2):
+        return remote(
+            gsend.at[j, c2],
+            grecv.at[s, c],
+            g_s.at[j, c2],
+            g_r.at[s, c],
+            {"seq": j, "ctx": c2},
+        )
+
+    def grad_piece(j):
+        cot_core(j, cot_all.at[j, :, c]).wait_recv()
+        for c2 in range(2):
+            block = cot_all[j, :, :, :, c2 * rows : (c2 + 1) * rows].reshape(-1, rows)
+            gsend[j, c2] = mm(comb_t[...], block).astype(BF)
+
+            @pl.when((j != s) | (c2 != c))
+            def _(c2=c2):
+                g_copy(j, c2).start()
+
+            @pl.when((j == s) & (c2 == c))
+            def _(c2=c2):
+                grecv[s, c] = gsend[s, c2]
+
+    def grad_step(t):
+        @pl.when(h - t >= 0)
+        def _():
+            grad_piece(h - t)
+
+        if t > 0:
+
+            @pl.when(h + t <= last)
+            def _():
+                grad_piece(h + t)
+
+    def fin_copy(index, ref):
+        return remote(ref.at[0, c], ref.at[0, c], fin_s.at[index], fin_r.at[index], {"ctx": o})
+
+    finals = [fin_copy(n, ref) for n, ref in enumerate((fin_ref, fgate_ref, fout_ref))]
+
+    fast_block(0)
+    combine(0)
+    gather_step(1)
+    project(0)
+    fast_block(1)
+    for copy in finals:
+        copy.start()
+    combine(1)
+    forward(0)
+    project(1)
+    grad_step(0)
+    for t in range(2, heads):
+        gather_step(t)
+        if t == 2:
+            forward(1)
+        grad_step(t - 1)
+    grad_step(heads - 1)
+    for b in range(blocks):
+        finish(b)
+    for copy in finals:
+        copy.wait()
+    for s2 in range(seqs):
+        for c2 in range(2):
+
+            @pl.when((s2 != s) | (c2 != c))
+            def _(s2=s2, c2=c2):
+                remote(
+                    gsend.at[s2, c2],
+                    grecv.at[s2, c2],
+                    g_s.at[s2, c2],
+                    g_r.at[s2, c2],
+                    {"ctx": o},
+                ).wait()
+
+    for i in range(2):
+        total = grecv[0, i].astype(F32)
+        for s2 in range(1, seqs):
+            total = total + grecv[s2, i].astype(F32)
+        grad_ref[i * dh : (i + 1) * dh, :] = total
+    for j in range(heads):
+        piece = cot_all.at[j, :, c]
+        cot_core(j, piece).wait_send()
+
+        @pl.when((j <= h) & (h < last))
+        def _(j=j, piece=piece):
+            cot_up(j, piece).wait_send()
+
+        @pl.when((j >= h) & (h > 0))
+        def _(j=j, piece=piece):
+            cot_down(j, piece).wait_send()
+
+
+def fused_shards(
+    queries,
+    key_vectors,
+    value_vectors,
+    token_rates,
+    fast_in,
+    fast_gate,
+    fast_out,
+    out_gain,
+    out_weight,
+    cotangent,
+):
+    seqs, heads = lax.axis_size("seq"), lax.axis_size("head")
+    local_heads, dh, fh = fast_in.shape
+    _, blocks, rows, width = queries.shape
+    depth = out_weight.shape[1]
+    vmem, dma = pltpu.VMEM, pltpu.SemaphoreType.DMA
+    whole = pl.BlockSpec(memory_space=pltpu.VMEM)
+    return pl.pallas_call(
+        functools.partial(layer_kernel, seqs, heads),
+        out_shape=(
+            jax.ShapeDtypeStruct((1, blocks, rows, width), BF),
+            jax.ShapeDtypeStruct((width, rows), F32),
+            jax.ShapeDtypeStruct((1, local_heads, dh, fh), F32),
+            jax.ShapeDtypeStruct((1, local_heads, dh, fh), F32),
+            jax.ShapeDtypeStruct((1, local_heads, fh, dh), F32),
+        ),
+        in_specs=[whole] * 10,
+        out_specs=(whole,) * 5,
+        scratch_shapes=[
+            vmem((blocks, 2, rows, dh), BF),
+            vmem((blocks, 2, rows, dh), BF),
+            vmem((blocks, 2, rows, dh), BF),
+            vmem((blocks, 2, rows, dh), BF),
+            vmem((blocks, rows, width), BF),
+            vmem((heads, blocks, 2, rows, width), BF),
+            vmem((dh, fh), BF),
+            vmem((dh, fh), BF),
+            vmem((fh, dh), BF),
+            vmem((dh, fh), F32),
+            vmem((dh, fh), F32),
+            vmem((fh, dh), F32),
+            vmem((2, rows, dh), F32),
+            vmem((blocks, 2, rows, dh), BF),
+            vmem((dh, blocks * 2 * rows), BF),
+            vmem((blocks, rows, width), BF),
+            vmem((blocks, heads, rows, width), BF),
+            vmem((blocks, heads, rows, width), BF),
+            vmem((blocks, heads, rows, width), BF),
+            vmem((heads, 2, dh, rows), BF),
+            vmem((seqs, 2, dh, rows), BF),
+            dma((4,)),
+            dma((4,)),
+            dma((heads,)),
+            dma((heads,)),
+            dma((heads,)),
+            dma((heads,)),
+            dma((heads,)),
+            dma((blocks,)),
+            dma((blocks,)),
+            dma((3,)),
+            dma((3,)),
+            dma((blocks, heads)),
+            dma((blocks, heads)),
+            dma((blocks, heads)),
+            dma((blocks, heads)),
+            dma((seqs, 2)),
+            dma((seqs, 2)),
+            dma((5,)),
+        ],
+        compiler_params=pltpu.CompilerParams(
+            collective_id=0, has_side_effects=True, vmem_limit_bytes=48 * 2**20
+        ),
+        cost_estimate=pl.CostEstimate(
+            flops=5 * 10**9, bytes_accessed=10 * 2**20, transcendentals=2 * 10**6
+        ),
+        name="layer",
+    )(
+        queries,
+        key_vectors,
+        value_vectors,
+        token_rates,
+        fast_in,
+        fast_gate,
+        fast_out,
+        out_gain.reshape(local_heads, dh),
+        out_weight,
+        cotangent,
+    )
+
+
+def pick(mesh):
+    fits = mesh.shape["ctx"] == 2 and mesh.shape["seq"] == mesh.shape["head"]
+
+    def body(*args):
+        local_heads, dh, _ = args[4].shape
+        _, _, rows, width = args[0].shape
+        square = dh == rows and width == 2 * rows and local_heads == 2
+        return (fused_shards if fits and square else shards)(*args)
+
+    return body
+
 
 def solution(mesh):
     return jax.shard_map(
-        shards,
+        pick(mesh),
         mesh=mesh,
         in_specs=(
             P("seq", None, "ctx", "head"),

time: 208 us -> 92.5 us (0.44)
  the two profiles are of different devices: /device:TPU:0 before, /device:TPU:7 now
where the time goes in v1:
time: 92.5 us; the launch traced here: 92 us
  Pallas kernels  78 us (84%)
  local copies, waits for them, and re-layouts  13.3 us (14%)
    pallas_call x1, Pallas kernels, fused_shards(): pl.pallas_call(functools.partial(layer_kernel, seqs, heads), out_shape=(j...  78 us
    unnamed x24, local copies, waits for them, and re-layouts  12.6 us

profile of v1, /device:TPU:7, one launch (start us, length us, event | category | flops | bytes accessed | tf_op | source)
XLA Modules:
  0.0 92.0 jit_solution(16419639936805101593)
XLA Ops:
  0.6 0.7 reshape.13.gain_ref
  1.3 0.8 copy.15.rate_ref
  2.2 0.0 copy-start
  2.2 1.0 %copy-done = bf16[1,2,256,512]{3,2,1,0:T(8,128)(2,1)S(1)} copy-done((bf16[1,2,256,512]{3,2,1,0:T(8,128)(2,1)S(1)}, bf16[1,2,256,512]{3,2,1,0:T(8,128)(2,1)}, u32[]{:S(2)}) %copy-start) | copy-done | bytes 524312
  3.2 0.0 copy-start.1
  3.2 1.0 %copy-done.1 = bf16[1,2,256,512]{3,2,1,0:T(8,128)(2,1)S(1)} copy-done((bf16[1,2,256,512]{3,2,1,0:T(8,128)(2,1)S(1)}, bf16[1,2,256,512]{3,2,1,0:T(8,128)(2,1)}, u32[]{:S(2)}) %copy-start.1) | copy-done | bytes 524312
  4.2 0.0 copy-start.2
  4.3 1.0 %copy-done.2 = bf16[1,2,256,512]{3,2,1,0:T(8,128)(2,1)S(1)} copy-done((bf16[1,2,256,512]{3,2,1,0:T(8,128)(2,1)S(1)}, bf16[1,2,256,512]{3,2,1,0:T(8,128)(2,1)}, u32[]{:S(2)}) %copy-start.2) | copy-done | bytes 524312
  5.3 0.0 copy-start.3
  5.3 1.0 %copy-done.3 = bf16[2,256,512]{2,1,0:T(8,128)(2,1)S(1)} copy-done((bf16[2,256,512]{2,1,0:T(8,128)(2,1)S(1)}, bf16[2,256,512]{2,1,0:T(8,128)(2,1)}, u32[]{:S(2)}) %copy-start.3) | copy-done | bytes 524312
  6.3 0.0 copy-start.4
  6.3 1.0 %copy-done.4 = bf16[2,256,512]{2,1,0:T(8,128)(2,1)S(1)} copy-done((bf16[2,256,512]{2,1,0:T(8,128)(2,1)S(1)}, bf16[2,256,512]{2,1,0:T(8,128)(2,1)}, u32[]{:S(2)}) %copy-start.4) | copy-done | bytes 524312
  7.4 0.0 copy-start.5
  7.4 1.0 %copy-done.5 = bf16[2,512,256]{2,1,0:T(8,128)(2,1)S(1)} copy-done((bf16[2,512,256]{2,1,0:T(8,128)(2,1)S(1)}, bf16[2,512,256]{2,1,0:T(8,128)(2,1)}, u32[]{:S(2)}) %copy-start.5) | copy-done | bytes 524312
  8.4 0.0 copy-start.6
  8.4 1.0 %copy-done.6 = bf16[1,2,256,512]{3,2,1,0:T(8,128)(2,1)S(1)} copy-done((bf16[1,2,256,512]{3,2,1,0:T(8,128)(2,1)S(1)}, bf16[1,2,256,512]{3,2,1,0:T(8,128)(2,1)}, u32[]{:S(2)}) %copy-start.6) | copy-done | bytes 524312
  9.5 78.0 %layer.1 = (bf16[1,2,256,512]{3,2,1,0:T(8,128)(2,1)S(1)}, f32[512,256]{1,0:T(8,128)S(1)}, f32[1,2,256,512]{3,2,1,0:T(8,128)S(1)}, f32[1,2,256,512]{3,2,1,0:T(8,128)}, f32[1,2,512,256]{3,2,1,0:T(8,128)}) custom-call(bf16[1,2,256,512]{3,2,1,0:T(8,128)(2,1)S(1)} %copy-done, bf16[1,2,256,512]{3,2,1,0:T(8,128)(2,1)S(1)} %copy-done.1, ...), custom_call_target="tpu_custom_call" | custom-call | flops 5000000000 | bytes 10485760 | tf_op jit(solution)/shard_map/layer/pallas_call | solution.py:629
  87.4 0.0 copy-start.8
  87.4 0.8 copy.21
  88.2 0.8 copy.22
  89.0 0.0 copy-start.7
  89.0 1.0 %copy.23 = f32[1,2,256,512]{3,2,1,0:T(8,128)} copy(f32[1,2,256,512]{3,2,1,0:T(8,128)S(1)} %get-tuple-element.12) | data formatting | bytes 2097152
  90.0 0.0 copy-done.8
  90.0 1.0 %copy.24 = f32[1,2,256,512]{3,2,1,0:T(8,128)} copy(f32[1,2,256,512]{3,2,1,0:T(8,128)S(1)} %copy-done.8) | data formatting | bytes 2097152
  91.0 0.0 copy-done.7
  91.0 1.0 %copy.25 = f32[1,2,512,256]{3,2,1,0:T(8,128)} copy(f32[1,2,512,256]{3,2,1,0:T(8,128)S(1)} %copy-done.7) | data formatting | bytes 2097152
Async XLA Ops:
  2.2 1.0 %copy-start = (bf16[1,2,256,512]{3,2,1,0:T(8,128)(2,1)S(1)}, bf16[1,2,256,512]{3,2,1,0:T(8,128)(2,1)}, u32[]{:S(2)}) copy-start(bf16[1,2,256,512]{3,2,1,0:T(8,128)(2,1)} %q_ref.1) | copy-start | bytes 1572868
  3.2 1.0 %copy-start.1 = (bf16[1,2,256,512]{3,2,1,0:T(8,128)(2,1)S(1)}, bf16[1,2,256,512]{3,2,1,0:T(8,128)(2,1)}, u32[]{:S(2)}) copy-start(bf16[1,2,256,512]{3,2,1,0:T(8,128)(2,1)} %k_ref.1) | copy-start | bytes 1572868
  4.2 1.0 %copy-start.2 = (bf16[1,2,256,512]{3,2,1,0:T(8,128)(2,1)S(1)}, bf16[1,2,256,512]{3,2,1,0:T(8,128)(2,1)}, u32[]{:S(2)}) copy-start(bf16[1,2,256,512]{3,2,1,0:T(8,128)(2,1)} %v_ref.1) | copy-start | bytes 1572868
  5.3 1.0 %copy-start.3 = (bf16[2,256,512]{2,1,0:T(8,128)(2,1)S(1)}, bf16[2,256,512]{2,1,0:T(8,128)(2,1)}, u32[]{:S(2)}) copy-start(bf16[2,256,512]{2,1,0:T(8,128)(2,1)} %win_ref.1) | copy-start | bytes 1572868
  6.3 1.0 %copy-start.4 = (bf16[2,256,512]{2,1,0:T(8,128)(2,1)S(1)}, bf16[2,256,512]{2,1,0:T(8,128)(2,1)}, u32[]{:S(2)}) copy-start(bf16[2,256,512]{2,1,0:T(8,128)(2,1)} %wgate_ref.1) | copy-start | bytes 1572868
  7.4 1.0 %copy-start.5 = (bf16[2,512,256]{2,1,0:T(8,128)(2,1)S(1)}, bf16[2,512,256]{2,1,0:T(8,128)(2,1)}, u32[]{:S(2)}) copy-start(bf16[2,512,256]{2,1,0:T(8,128)(2,1)} %wout_ref.1) | copy-start | bytes 1572868
  8.4 1.0 %copy-start.6 = (bf16[1,2,256,512]{3,2,1,0:T(8,128)(2,1)S(1)}, bf16[1,2,256,512]{3,2,1,0:T(8,128)(2,1)}, u32[]{:S(2)}) copy-start(bf16[1,2,256,512]{3,2,1,0:T(8,128)(2,1)} %cot_ref.1) | copy-start | bytes 1572868
  87.4 2.6 %copy-start.8 = (f32[1,2,256,512]{3,2,1,0:T(8,128)S(1)}, f32[1,2,256,512]{3,2,1,0:T(8,128)}, u32[]{:S(2)}) copy-start(f32[1,2,256,512]{3,2,1,0:T(8,128)} %get-tuple-element.13) | copy-start | bytes 3145732
  89.0 1.9 %copy-start.7 = (f32[1,2,512,256]{3,2,1,0:T(8,128)S(1)}, f32[1,2,512,256]{3,2,1,0:T(8,128)}, u32[]{:S(2)}) copy-start(f32[1,2,512,256]{3,2,1,0:T(8,128)} %get-tuple-element.14) | copy-start | bytes 3145732

commit v2 on v1

--- a/solution.py
+++ b/solution.py
@@ -207,6 +207,16 @@
     down_buf,
     gsend,
     grecv,
+    last_in,
+    last_gate,
+    last_out,
+    layer,
+    grad,
+    v_own,
+    weights_in,
+    weights_gate,
+    weights_out,
+    ow_own,
     core_s,
     core_r,
     cot_core_s,
@@ -246,6 +256,23 @@
             device_id_type=pl.DeviceIdType.MESH,
         )
 
+    fetches = [
+        pltpu.make_async_copy(src, dst, local_s.at[n])
+        for n, (src, dst) in enumerate(
+            (
+                (v_ref.at[0], v_own),
+                (win_ref.at[c], weights_in),
+                (wgate_ref.at[c], weights_gate),
+                (wout_ref.at[c], weights_out),
+                (ow_ref, ow_own),
+            ),
+            5,
+        )
+    ]
+    for copy in fetches:
+        copy.start()
+    fetch_v, *fetch_weights, fetch_ow = fetches
+
     barrier = pltpu.get_barrier_semaphore()
     for s2 in range(seqs):
         for c2 in range(2):
@@ -273,6 +300,12 @@
 
     ends = (h == 0).astype(jnp.int32) + (h == last).astype(jnp.int32)
     pl.semaphore_wait(barrier, 2 * seqs - 1 + 2 - ends)
+
+    writes = []
+
+    def write(src, dst, index):
+        writes.append(pltpu.make_async_copy(src, dst, local_s.at[index]))
+        writes[-1].start()
 
     def cot_up(owner, src):
         return remote(
@@ -310,11 +343,12 @@
     def _():
         cot_down(h, cot_ref.at[0]).start()
 
+    fetch_v.wait()
     for b in range(blocks):
         for i in range(2):
             cols = slice(i * dh, (i + 1) * dh)
-            rate = rate_ref[0, b, :, i : i + 1]
-            sv_all[b, :, cols] = (rate * v_ref[0, b, :, cols].astype(F32)).astype(BF)
+            rate = jnp.broadcast_to(rate_ref[0, b, i : i + 1, :], (128, rows)).T[:, :1]
+            sv_all[b, :, cols] = (rate * v_own[b, :, cols].astype(F32)).astype(BF)
     swaps[1].start()
     cot_core(h, cot_ref.at[0]).start()
     locals_ = [
@@ -331,9 +365,11 @@
         return jnp.sum(weight * weight, axis=0, keepdims=True) + 1e-06
 
     targets = []
-    for src, kept in ((win_ref, rin), (wgate_ref, rgate), (wout_ref, rout)):
-        kept[...] = src[c]
-        targets.append(jnp.sqrt(squares(src[c].astype(F32))))
+    for copy in fetch_weights:
+        copy.wait()
+    for src, kept in ((weights_in, rin), (weights_gate, rgate), (weights_out, rout)):
+        kept[...] = src[...]
+        targets.append(jnp.sqrt(squares(src[...].astype(F32))))
     for copy in locals_:
         copy.wait()
     for copy in swaps:
@@ -374,13 +410,13 @@
             fast[i] = mm(hidden, rout[...])
 
         for kept, acc, final, target, start in (
-            (rin, acc_in, fin_ref, targets[0], win_ref),
-            (rgate, acc_gate, fgate_ref, targets[1], wgate_ref),
-            (rout, acc_out, fout_ref, targets[2], wout_ref),
+            (rin, acc_in, last_in, targets[0], weights_in),
+            (rgate, acc_gate, last_gate, targets[1], weights_gate),
+            (rout, acc_out, last_out, targets[2], weights_out),
         ):
-            weight = (start[c].astype(F32) if b == 0 else final[0, c]) + acc[...]
+            weight = (start[...].astype(F32) if b == 0 else final[...]) + acc[...]
             weight = weight * (target / jnp.sqrt(squares(weight)))
-            final[0, c] = weight
+            final[...] = weight
             kept[...] = weight.astype(BF)
 
     row = lax.broadcasted_iota(jnp.int32, (rows, rows), 0)
@@ -415,7 +451,7 @@
     def combine(b):
         for i in range(2):
             value = (
-                normalize_rms(fast[i], 1e-05) * gain_ref[pl.ds(c, 1), :] + attend(b, i)
+                normalize_rms(fast[i], 1e-05) * gain_ref[:, mine] + attend(b, i)
             ).astype(BF)
             comb[b, i] = value
             at = (b * 2 + i) * rows
@@ -423,7 +459,7 @@
         comb_copy(b).start()
         own[b, :, mine] = comb[b, c]
 
-    width = ow_ref.shape[1] // heads
+    width = ow_own.shape[1] // heads
 
     def up_copy(b, d):
         return remote(
@@ -439,7 +475,7 @@
         comb_copy(b).wait()
         rows_in = own[b]
         for d in range(heads):
-            part[b, d] = mm(rows_in, ow_ref[:, d * width : (d + 1) * width]).astype(BF)
+            part[b, d] = mm(rows_in, ow_own[:, d * width : (d + 1) * width]).astype(BF)
 
         @pl.when(h == 0)
         def _():
@@ -455,18 +491,18 @@
         part[b, d] = (part[b, d].astype(F32) + buf[b, d].astype(F32)).astype(BF)
 
     def forward(b):
-        for step in range(heads - 2):
-            d = last - step
-
-            @pl.when((h > 0) & (h < d))
+        for step in range(1, last):
+            d = last + h - step
+
+            @pl.when((h > 0) & (d <= last))
             def _(d=d):
                 up_copy(b, d).wait_recv()
                 add(b, d, up_buf)
                 up_copy(b, d).start()
 
-            e = step
-
-            @pl.when((h < last) & (h > e))
+            e = step - (last - h)
+
+            @pl.when((h < last) & (e >= 0))
             def _(e=e):
                 down_copy(b, e).wait_recv()
                 add(b, e, down_buf)
@@ -483,7 +519,8 @@
             down_copy(b, h).wait_recv()
             add(b, h, down_buf)
 
-        out_ref[0, b] = part[b, h]
+        layer[b] = part[b, h]
+        write(layer.at[b], out_ref.at[0, b], 13 + b)
         for d in range(heads):
 
             @pl.when(d > h)
@@ -551,27 +588,31 @@
             def _():
                 grad_piece(h + t)
 
-    def fin_copy(index, ref):
-        return remote(ref.at[0, c], ref.at[0, c], fin_s.at[index], fin_r.at[index], {"ctx": o})
-
-    finals = [fin_copy(n, ref) for n, ref in enumerate((fin_ref, fgate_ref, fout_ref))]
+    results = ((last_in, fin_ref), (last_gate, fgate_ref), (last_out, fout_ref))
+    finals = [
+        remote(src, dst.at[0, c], fin_s.at[n], fin_r.at[n], {"ctx": o})
+        for n, (src, dst) in enumerate(results)
+    ]
 
     fast_block(0)
     combine(0)
     gather_step(1)
+    fetch_ow.wait()
     project(0)
     fast_block(1)
     for copy in finals:
         copy.start()
+    for n, (src, dst) in enumerate(results):
+        write(src, dst.at[0, c], 10 + n)
     combine(1)
-    forward(0)
     project(1)
     grad_step(0)
     for t in range(2, heads):
+        grad_step(t - 1)
         gather_step(t)
         if t == 2:
+            forward(0)
             forward(1)
-        grad_step(t - 1)
     grad_step(heads - 1)
     for b in range(blocks):
         finish(b)
@@ -591,10 +632,12 @@
                 ).wait()
 
     for i in range(2):
+        span = pl.ds(i * dh, dh)
         total = grecv[0, i].astype(F32)
         for s2 in range(1, seqs):
             total = total + grecv[s2, i].astype(F32)
-        grad_ref[i * dh : (i + 1) * dh, :] = total
+        grad[span, :] = total
+        write(grad.at[span, :], grad_ref.at[span, :], 13 + blocks + i)
     for j in range(heads):
         piece = cot_all.at[j, :, c]
         cot_core(j, piece).wait_send()
@@ -606,6 +649,27 @@
         @pl.when((j >= h) & (h > 0))
         def _(j=j, piece=piece):
             cot_down(j, piece).wait_send()
+
+    for copy in writes:
+        copy.wait()
+
+
+def write_kernel(*refs):
+    count = len(refs) // 2
+    sources, targets, sems = refs[:count], refs[count:-1], refs[-1]
+    copies = []
+    for src, dst in zip(sources, targets):
+        if len(src.shape) == 2:
+            span = src.shape[0] // 2
+            parts = [pl.ds(i * span, span) for i in range(2)]
+        else:
+            parts = [(0, i) for i in range(2)]
+        for at in parts:
+            one, other = src.at[at], dst.at[at]
+            copies.append(pltpu.make_async_copy(one, other, sems.at[len(copies)]))
+            copies[-1].start()
+    for copy in copies:
+        copy.wait()
 
 
 def fused_shards(
@@ -626,17 +690,19 @@
     depth = out_weight.shape[1]
     vmem, dma = pltpu.VMEM, pltpu.SemaphoreType.DMA
     whole = pl.BlockSpec(memory_space=pltpu.VMEM)
-    return pl.pallas_call(
+    hbm = pl.BlockSpec(memory_space=pl.ANY)
+    shapes = (
+        jax.ShapeDtypeStruct((1, blocks, rows, width), BF),
+        jax.ShapeDtypeStruct((width, rows), F32),
+        jax.ShapeDtypeStruct((1, local_heads, dh, fh), F32),
+        jax.ShapeDtypeStruct((1, local_heads, dh, fh), F32),
+        jax.ShapeDtypeStruct((1, local_heads, fh, dh), F32),
+    )
+    results = pl.pallas_call(
         functools.partial(layer_kernel, seqs, heads),
-        out_shape=(
-            jax.ShapeDtypeStruct((1, blocks, rows, width), BF),
-            jax.ShapeDtypeStruct((width, rows), F32),
-            jax.ShapeDtypeStruct((1, local_heads, dh, fh), F32),
-            jax.ShapeDtypeStruct((1, local_heads, dh, fh), F32),
-            jax.ShapeDtypeStruct((1, local_heads, fh, dh), F32),
-        ),
-        in_specs=[whole] * 10,
-        out_specs=(whole,) * 5,
+        out_shape=shapes,
+        in_specs=[hbm, hbm, hbm, whole, hbm, hbm, hbm, whole, hbm, hbm],
+        out_specs=(hbm,) * 5,
         scratch_shapes=[
             vmem((blocks, 2, rows, dh), BF),
             vmem((blocks, 2, rows, dh), BF),
@@ -659,6 +725,16 @@
             vmem((blocks, heads, rows, width), BF),
             vmem((heads, 2, dh, rows), BF),
             vmem((seqs, 2, dh, rows), BF),
+            vmem((dh, fh), F32),
+            vmem((dh, fh), F32),
+            vmem((fh, dh), F32),
+            vmem((blocks, rows, width), BF),
+            vmem((width, rows), F32),
+            vmem((blocks, rows, width), BF),
+            vmem((dh, fh), BF),
+            vmem((dh, fh), BF),
+            vmem((fh, dh), BF),
+            vmem((width, depth), BF),
             dma((4,)),
             dma((4,)),
             dma((heads,)),
@@ -676,10 +752,10 @@
             dma((blocks, heads)),
             dma((seqs, 2)),
             dma((seqs, 2)),
-            dma((5,)),
+            dma((15 + blocks,)),
         ],
         compiler_params=pltpu.CompilerParams(
-            collective_id=0, has_side_effects=True, vmem_limit_bytes=48 * 2**20
+            collective_id=0, has_side_effects=True, vmem_limit_bytes=60 * 2**20
         ),
         cost_estimate=pl.CostEstimate(
             flops=5 * 10**9, bytes_accessed=10 * 2**20, transcendentals=2 * 10**6
@@ -689,14 +765,23 @@
         queries,
         key_vectors,
         value_vectors,
-        token_rates,
+        jnp.swapaxes(token_rates, 2, 3),
         fast_in,
         fast_gate,
         fast_out,
-        out_gain.reshape(local_heads, dh),
+        out_gain.reshape(1, width),
         out_weight,
         cotangent,
     )
+    return pl.pallas_call(
+        write_kernel,
+        out_shape=shapes,
+        in_specs=[hbm] * 5,
+        out_specs=(hbm,) * 5,
+        scratch_shapes=[dma((10,))],
+        compiler_params=pltpu.CompilerParams(vmem_limit_bytes=60 * 2**20),
+        name="write",
+    )(*results)
 
 
 def pick(mesh):
@@ -705,7 +790,7 @@
     def body(*args):
         local_heads, dh, _ = args[4].shape
         _, _, rows, width = args[0].shape
-        square = dh == rows and width == 2 * rows and local_heads == 2
+        square = dh == rows and width == 2 * rows and local_heads == 2 and args[0].shape[1] == 2
         return (fused_shards if fits and square else shards)(*args)
 
     return body

time: 92.5 us -> 192 us (2.08)
  the two profiles are of different devices: /device:TPU:7 before, /device:TPU:0 now
where the time goes in v2:
time: 192 us; the launch traced here: 190 us
  Pallas kernels  189 us (98%)
    pallas_call x1, Pallas kernels, fused_shards(): pl.pallas_call(write_kernel, out_shape=shapes, in_specs=[hbm] * 5, out_sp...  128 us
    pallas_call x1, Pallas kernels, fused_shards(): pl.pallas_call(functools.partial(layer_kernel, seqs, heads), out_shape=sh...  60.9 us

profile of v2, /device:TPU:0, one launch (start us, length us, event | category | flops | bytes accessed | tf_op | source)
XLA Modules:
  0.0 189.8 jit_solution(18233657337431735057)
XLA Ops:
  0.6 60.9 %layer.1 = (bf16[1,2,256,512]{3,2,1,0:T(8,128)(2,1)}, f32[512,256]{1,0:T(8,128)}, f32[1,2,256,512]{3,2,1,0:T(8,128)}, f32[1,2,256,512]{3,2,1,0:T(8,128)}, f32[1,2,512,256]{3,2,1,0:T(8,128)}) custom-call(bf16[1,2,256,512]{3,2,1,0:T(8,128)(2,1)} %q_ref.1, bf16[1,2,256,512]{3,2,1,0:T(8,128)(2,1)} %k_ref.1, bf16[1,2,256,512]{3,2,1,0:T(8,128)(2,1)} %v_ref.1, ...), custom_call_target="tpu_custom_call" | custom-call | flops 5000000000 | bytes 10485760 | tf_op jit(solution)/shard_map/layer/pallas_call | solution.py:701
  61.6 128.3 %write.1 = (bf16[1,2,256,512]{3,2,1,0:T(8,128)(2,1)}, f32[512,256]{1,0:T(8,128)}, f32[1,2,256,512]{3,2,1,0:T(8,128)}, f32[1,2,256,512]{3,2,1,0:T(8,128)}, f32[1,2,512,256]{3,2,1,0:T(8,128)}) custom-call(bf16[1,2,256,512]{3,2,1,0:T(8,128)(2,1)} %get-tuple-element.10.refs_0_, f32[512,256]{1,0:T(8,128)} %get-tuple-element.11.refs_1_, ...), custom_call_target="tpu_custom_call" | custom-call | tf_op jit(solution)/shard_map/write/pallas_call | solution.py:776

commit v3 on v2

--- a/solution.py
+++ b/solution.py
@@ -375,7 +375,15 @@
     for copy in swaps:
         copy.wait()
 
-    def fast_block(b):
+    def query_block(b):
+        @pl.loop(0, 2)
+        def _(i):
+            query_norm = normalize_rms(qh[b, i].astype(F32), 1e-05).astype(BF)
+            first = mm(query_norm, rin[...])
+            hidden = (first * jax.nn.sigmoid(first) * mm(query_norm, rgate[...])).astype(BF)
+            fast[i] = mm(hidden, rout[...])
+
+    def key_block(b):
         @pl.loop(0, 2)
         def _(i):
             key_norm = normalize_rms(kh[b, i].astype(F32), 1e-05).astype(BF)
@@ -404,11 +412,6 @@
                 acc_gate[...] += up_gate
                 acc_out[...] += up_out
 
-            query_norm = normalize_rms(qh[b, i].astype(F32), 1e-05).astype(BF)
-            first = mm(query_norm, rin[...])
-            hidden = (first * jax.nn.sigmoid(first) * mm(query_norm, rgate[...])).astype(BF)
-            fast[i] = mm(hidden, rout[...])
-
         for kept, acc, final, target, start in (
             (rin, acc_in, last_in, targets[0], weights_in),
             (rgate, acc_gate, last_gate, targets[1], weights_gate),
@@ -594,26 +597,29 @@
         for n, (src, dst) in enumerate(results)
     ]
 
-    fast_block(0)
+    query_block(0)
     combine(0)
-    gather_step(1)
     fetch_ow.wait()
     project(0)
-    fast_block(1)
+    key_block(0)
+    gather_step(1)
+    query_block(1)
+    combine(1)
+    project(1)
+    grad_step(0)
+    grad_step(1)
+    key_block(1)
     for copy in finals:
         copy.start()
     for n, (src, dst) in enumerate(results):
         write(src, dst.at[0, c], 10 + n)
-    combine(1)
-    project(1)
-    grad_step(0)
     for t in range(2, heads):
-        grad_step(t - 1)
         gather_step(t)
         if t == 2:
             forward(0)
+        grad_step(t)
+        if t == 2:
             forward(1)
-    grad_step(heads - 1)
     for b in range(blocks):
         finish(b)
     for copy in finals:
@@ -655,21 +661,25 @@
 
 
 def write_kernel(*refs):
-    count = len(refs) // 2
-    sources, targets, sems = refs[:count], refs[count:-1], refs[-1]
-    copies = []
-    for src, dst in zip(sources, targets):
+    count = len(refs) // 3
+    sems = refs[-1]
+    reads, writes = [], []
+    for src, dst, held in zip(refs[:count], refs[count : 2 * count], refs[2 * count : -1]):
         if len(src.shape) == 2:
             span = src.shape[0] // 2
             parts = [pl.ds(i * span, span) for i in range(2)]
         else:
             parts = [(0, i) for i in range(2)]
         for at in parts:
-            one, other = src.at[at], dst.at[at]
-            copies.append(pltpu.make_async_copy(one, other, sems.at[len(copies)]))
-            copies[-1].start()
-    for copy in copies:
-        copy.wait()
+            n = len(reads)
+            reads.append(pltpu.make_async_copy(src.at[at], held.at[at], sems.at[0, n]))
+            writes.append(pltpu.make_async_copy(held.at[at], dst.at[at], sems.at[1, n]))
+            reads[-1].start()
+    for read, write in zip(reads, writes):
+        read.wait()
+        write.start()
+    for write in writes:
+        write.wait()
 
 
 def fused_shards(
@@ -778,7 +788,7 @@
         out_shape=shapes,
         in_specs=[hbm] * 5,
         out_specs=(hbm,) * 5,
-        scratch_shapes=[dma((10,))],
+        scratch_shapes=[vmem(shape.shape, shape.dtype) for shape in shapes] + [dma((2, 10))],
         compiler_params=pltpu.CompilerParams(vmem_limit_bytes=60 * 2**20),
         name="write",
     )(*results)

time: 192 us -> 66.5 us (0.35); the launches traced: 190 us -> 66.3 us
  Pallas kernels: 189 us -> 65.7 us
    pallas_call x1, Pallas kernels: 128 us -> 3.85 us  [fused_shards(): pl.pallas_call(write_kernel, out_shape=shapes, in_specs=[hbm] * 5, out_sp...]
where the time goes in v3:
time: 66.5 us; the launch traced here: 66.3 us
  Pallas kernels  65.7 us (99%)
    pallas_call x1, Pallas kernels, fused_shards(): pl.pallas_call(functools.partial(layer_kernel, seqs, heads), out_shape=sh...  61.8 us
    pallas_call x1, Pallas kernels, fused_shards(): pl.pallas_call(write_kernel, out_shape=shapes, in_specs=[hbm] * 5, out_sp...  3.85 us

profile of v3, /device:TPU:0, one launch (start us, length us, event | category | flops | bytes accessed | tf_op | source)
XLA Modules:
  0.0 66.3 jit_solution(4347976306562352527)
XLA Ops:
  0.6 61.8 %layer.1 = (bf16[1,2,256,512]{3,2,1,0:T(8,128)(2,1)}, f32[512,256]{1,0:T(8,128)}, f32[1,2,256,512]{3,2,1,0:T(8,128)}, f32[1,2,256,512]{3,2,1,0:T(8,128)}, f32[1,2,512,256]{3,2,1,0:T(8,128)}) custom-call(bf16[1,2,256,512]{3,2,1,0:T(8,128)(2,1)} %q_ref.1, bf16[1,2,256,512]{3,2,1,0:T(8,128)(2,1)} %k_ref.1, bf16[1,2,256,512]{3,2,1,0:T(8,128)(2,1)} %v_ref.1, ...), custom_call_target="tpu_custom_call" | custom-call | flops 5000000000 | bytes 10485760 | tf_op jit(solution)/shard_map/layer/pallas_call | solution.py:711
  62.5 3.9 %write.1 = (bf16[1,2,256,512]{3,2,1,0:T(8,128)(2,1)}, f32[512,256]{1,0:T(8,128)}, f32[1,2,256,512]{3,2,1,0:T(8,128)}, f32[1,2,256,512]{3,2,1,0:T(8,128)}, f32[1,2,512,256]{3,2,1,0:T(8,128)}) custom-call(bf16[1,2,256,512]{3,2,1,0:T(8,128)(2,1)} %get-tuple-element.10.refs_0_, f32[512,256]{1,0:T(8,128)} %get-tuple-element.11.refs_1_, ...), custom_call_target="tpu_custom_call" | custom-call | tf_op jit(solution)/shard_map/write/pallas_call | solution.py:786

commit v4 on v3

--- a/solution.py
+++ b/solution.py
@@ -307,14 +307,24 @@
         writes.append(pltpu.make_async_copy(src, dst, local_s.at[index]))
         writes[-1].start()
 
-    def cot_up(owner, src):
+    def cot_up(owner, b, src=None):
+        place = cot_all.at[owner, b, c]
         return remote(
-            src, cot_all.at[owner, :, c], ag_up_s.at[owner], ag_r.at[owner], {"head": h + 1}
-        )
-
-    def cot_down(owner, src):
+            place if src is None else src,
+            place,
+            ag_up_s.at[owner, b],
+            ag_r.at[owner, b],
+            {"head": h + 1},
+        )
+
+    def cot_down(owner, b, src=None):
+        place = cot_all.at[owner, b, c]
         return remote(
-            src, cot_all.at[owner, :, c], ag_down_s.at[owner], ag_r.at[owner], {"head": h - 1}
+            place if src is None else src,
+            place,
+            ag_down_s.at[owner, b],
+            ag_r.at[owner, b],
+            {"head": h - 1},
         )
 
     def cot_core(owner, src):
@@ -337,11 +347,13 @@
 
     @pl.when(h < last)
     def _():
-        cot_up(h, cot_ref.at[0]).start()
+        for b in range(blocks):
+            cot_up(h, b, cot_ref.at[0, b]).start()
 
     @pl.when(h > 0)
     def _():
-        cot_down(h, cot_ref.at[0]).start()
+        for b in range(blocks):
+            cot_down(h, b, cot_ref.at[0, b]).start()
 
     fetch_v.wait()
     for b in range(blocks):
@@ -480,14 +492,39 @@
         for d in range(heads):
             part[b, d] = mm(rows_in, ow_own[:, d * width : (d + 1) * width]).astype(BF)
 
+    def drain_up():
+        for j in range(last):
+            for b in range(blocks):
+
+                @pl.when(j <= h)
+                def _(j=j, b=b):
+                    cot_up(j, b).wait_send()
+
+    def drain_down():
+        for j in range(1, heads):
+            for b in range(blocks):
+
+                @pl.when(j >= h)
+                def _(j=j, b=b):
+                    cot_down(j, b).wait_send()
+
+    def release(b):
         @pl.when(h == 0)
         def _():
+            if b == 0:
+                drain_up()
             for d in range(last, 0, -1):
+                if b > 0:
+                    up_copy(b - 1, d).wait_send()
                 up_copy(b, d).start()
 
         @pl.when(h == last)
         def _():
+            if b == 0:
+                drain_down()
             for d in range(last):
+                if b > 0:
+                    down_copy(b - 1, d).wait_send()
                 down_copy(b, d).start()
 
     def add(b, d, buf):
@@ -501,6 +538,12 @@
             def _(d=d):
                 up_copy(b, d).wait_recv()
                 add(b, d, up_buf)
+                if b == 0:
+
+                    @pl.when(d == last)
+                    def _():
+                        drain_up()
+
                 up_copy(b, d).start()
 
             e = step - (last - h)
@@ -509,6 +552,12 @@
             def _(e=e):
                 down_copy(b, e).wait_recv()
                 add(b, e, down_buf)
+                if b == 0:
+
+                    @pl.when(e == 0)
+                    def _():
+                        drain_down()
+
                 down_copy(b, e).start()
 
     def finish(b):
@@ -526,36 +575,38 @@
         write(layer.at[b], out_ref.at[0, b], 13 + b)
         for d in range(heads):
 
-            @pl.when(d > h)
+            @pl.when((d > h) & (h > 0 if b < blocks - 1 else h >= 0))
             def _(d=d):
                 up_copy(b, d).wait_send()
 
-            @pl.when(d < h)
+            @pl.when((d < h) & (h < last if b < blocks - 1 else h <= last))
             def _(d=d):
                 down_copy(b, d).wait_send()
 
-    def gather_step(t):
+    def gather_step(t, b):
         @pl.when(h - t >= 0)
         def _():
             owner = h - t
-            piece = cot_all.at[owner, :, c]
-            cot_up(owner, piece).wait_recv()
-            cot_core(owner, piece).start()
+            cot_up(owner, b).wait_recv()
 
             @pl.when(h < last)
             def _():
-                cot_up(owner, piece).start()
+                cot_up(owner, b).start()
+
+            if b == blocks - 1:
+                cot_core(owner, cot_all.at[owner, :, c]).start()
 
         @pl.when(h + t <= last)
         def _():
             owner = h + t
-            piece = cot_all.at[owner, :, c]
-            cot_down(owner, piece).wait_recv()
-            cot_core(owner, piece).start()
+            cot_down(owner, b).wait_recv()
 
             @pl.when(h > 0)
             def _():
-                cot_down(owner, piece).start()
+                cot_down(owner, b).start()
+
+            if b == blocks - 1:
+                cot_core(owner, cot_all.at[owner, :, c]).start()
 
     def g_copy(j, c2):
         return remote(
@@ -599,12 +650,16 @@
 
     query_block(0)
     combine(0)
+    gather_step(1, 0)
     fetch_ow.wait()
     project(0)
     key_block(0)
-    gather_step(1)
+    gather_step(1, 1)
+    release(0)
     query_block(1)
     combine(1)
+    if last > 2:
+        gather_step(2, 0)
     project(1)
     grad_step(0)
     grad_step(1)
@@ -613,13 +668,19 @@
         copy.start()
     for n, (src, dst) in enumerate(results):
         write(src, dst.at[0, c], 10 + n)
-    for t in range(2, heads):
-        gather_step(t)
-        if t == 2:
-            forward(0)
+    for t in range(2, last):
+        if t > 2:
+            gather_step(t, 0)
+        gather_step(t, 1)
+    forward(0)
+    for t in range(2, last):
         grad_step(t)
-        if t == 2:
-            forward(1)
+    release(1)
+    forward(1)
+    if last > 1:
+        gather_step(last, 0)
+        gather_step(last, 1)
+        grad_step(last)
     for b in range(blocks):
         finish(b)
     for copy in finals:
@@ -647,14 +708,6 @@
     for j in range(heads):
         piece = cot_all.at[j, :, c]
         cot_core(j, piece).wait_send()
-
-        @pl.when((j <= h) & (h < last))
-        def _(j=j, piece=piece):
-            cot_up(j, piece).wait_send()
-
-        @pl.when((j >= h) & (h > 0))
-        def _(j=j, piece=piece):
-            cot_down(j, piece).wait_send()
 
     for copy in writes:
         copy.wait()
@@ -749,9 +802,9 @@
             dma((4,)),
             dma((heads,)),
             dma((heads,)),
-            dma((heads,)),
-            dma((heads,)),
-            dma((heads,)),
+            dma((heads, blocks)),
+            dma((heads, blocks)),
+            dma((heads, blocks)),
             dma((blocks,)),
             dma((blocks,)),
             dma((3,)),

time: 66.5 us -> 66.3 us (level)
  no operation moved by 1% of the time
where the time goes in v4:
time: 66.3 us; the launch traced here: 66.1 us
  Pallas kernels  65.5 us (99%)
    pallas_call x1, Pallas kernels, fused_shards(): pl.pallas_call(functools.partial(layer_kernel, seqs, heads), out_shape=sh...  61.6 us
    pallas_call x1, Pallas kernels, fused_shards(): pl.pallas_call(write_kernel, out_shape=shapes, in_specs=[hbm] * 5, out_sp...  3.85 us

profile of v4, /device:TPU:0, one launch (start us, length us, event | category | flops | bytes accessed | tf_op | source)
XLA Modules:
  0.0 66.1 jit_solution(3952690938834591050)
XLA Ops:
  0.6 61.6 %layer.1 = (bf16[1,2,256,512]{3,2,1,0:T(8,128)(2,1)}, f32[512,256]{1,0:T(8,128)}, f32[1,2,256,512]{3,2,1,0:T(8,128)}, f32[1,2,256,512]{3,2,1,0:T(8,128)}, f32[1,2,512,256]{3,2,1,0:T(8,128)}) custom-call(bf16[1,2,256,512]{3,2,1,0:T(8,128)(2,1)} %q_ref.1, bf16[1,2,256,512]{3,2,1,0:T(8,128)(2,1)} %k_ref.1, bf16[1,2,256,512]{3,2,1,0:T(8,128)(2,1)} %v_ref.1, ...), custom_call_target="tpu_custom_call" | custom-call | flops 5000000000 | bytes 10485760 | tf_op jit(solution)/shard_map/layer/pallas_call | solution.py:764
  62.3 3.9 %write.1 = (bf16[1,2,256,512]{3,2,1,0:T(8,128)(2,1)}, f32[512,256]{1,0:T(8,128)}, f32[1,2,256,512]{3,2,1,0:T(8,128)}, f32[1,2,256,512]{3,2,1,0:T(8,128)}, f32[1,2,512,256]{3,2,1,0:T(8,128)}) custom-call(bf16[1,2,256,512]{3,2,1,0:T(8,128)(2,1)} %get-tuple-element.10.refs_0_, f32[512,256]{1,0:T(8,128)} %get-tuple-element.11.refs_1_, ...), custom_call_target="tpu_custom_call" | custom-call | tf_op jit(solution)/shard_map/write/pallas_call | solution.py:839

commit v5 on v4

--- a/solution.py
+++ b/solution.py
@@ -514,8 +514,6 @@
             if b == 0:
                 drain_up()
             for d in range(last, 0, -1):
-                if b > 0:
-                    up_copy(b - 1, d).wait_send()
                 up_copy(b, d).start()
 
         @pl.when(h == last)
@@ -523,42 +521,39 @@
             if b == 0:
                 drain_down()
             for d in range(last):
-                if b > 0:
-                    down_copy(b - 1, d).wait_send()
                 down_copy(b, d).start()
 
     def add(b, d, buf):
         part[b, d] = (part[b, d].astype(F32) + buf[b, d].astype(F32)).astype(BF)
 
-    def forward(b):
-        for step in range(1, last):
-            d = last + h - step
-
-            @pl.when((h > 0) & (d <= last))
-            def _(d=d):
-                up_copy(b, d).wait_recv()
-                add(b, d, up_buf)
-                if b == 0:
-
-                    @pl.when(d == last)
-                    def _():
-                        drain_up()
-
-                up_copy(b, d).start()
-
-            e = step - (last - h)
-
-            @pl.when((h < last) & (e >= 0))
-            def _(e=e):
-                down_copy(b, e).wait_recv()
-                add(b, e, down_buf)
-                if b == 0:
-
-                    @pl.when(e == 0)
-                    def _():
-                        drain_down()
-
-                down_copy(b, e).start()
+    def forward(b, step):
+        d = last + h - step
+
+        @pl.when((h > 0) & (d <= last))
+        def _(d=d):
+            up_copy(b, d).wait_recv()
+            add(b, d, up_buf)
+            if b == 0:
+
+                @pl.when(d == last)
+                def _():
+                    drain_up()
+
+            up_copy(b, d).start()
+
+        e = step - (last - h)
+
+        @pl.when((h < last) & (e >= 0))
+        def _(e=e):
+            down_copy(b, e).wait_recv()
+            add(b, e, down_buf)
+            if b == 0:
+
+                @pl.when(e == 0)
+                def _():
+                    drain_down()
+
+            down_copy(b, e).start()
 
     def finish(b):
         @pl.when(h > 0)
@@ -575,11 +570,11 @@
         write(layer.at[b], out_ref.at[0, b], 13 + b)
         for d in range(heads):
 
-            @pl.when((d > h) & (h > 0 if b < blocks - 1 else h >= 0))
+            @pl.when(d > h)
             def _(d=d):
                 up_copy(b, d).wait_send()
 
-            @pl.when((d < h) & (h < last if b < blocks - 1 else h <= last))
+            @pl.when(d < h)
             def _(d=d):
                 down_copy(b, d).wait_send()
 
@@ -653,30 +648,34 @@
     gather_step(1, 0)
     fetch_ow.wait()
     project(0)
-    key_block(0)
     gather_step(1, 1)
     release(0)
+    key_block(0)
     query_block(1)
     combine(1)
     if last > 2:
         gather_step(2, 0)
     project(1)
+    release(1)
     grad_step(0)
+    for t in range(2, last):
+        if t > 2:
+            gather_step(t, 0)
+        gather_step(t, 1)
     grad_step(1)
+    if last > 1:
+        forward(0, 1)
     key_block(1)
     for copy in finals:
         copy.start()
     for n, (src, dst) in enumerate(results):
         write(src, dst.at[0, c], 10 + n)
-    for t in range(2, last):
-        if t > 2:
-            gather_step(t, 0)
-        gather_step(t, 1)
-    forward(0)
+    for step in range(2, last):
+        forward(0, step)
     for t in range(2, last):
         grad_step(t)
-    release(1)
-    forward(1)
+    for step in range(1, last):
+        forward(1, step)
     if last > 1:
         gather_step(last, 0)
         gather_step(last, 1)

time: 66.3 us -> 66.5 us (level)
  no operation moved by 1% of the time
where the time goes in v5:
time: 66.5 us; the launch traced here: 66.3 us
  Pallas kernels  65.7 us (99%)
    pallas_call x1, Pallas kernels, fused_shards(): pl.pallas_call(functools.partial(layer_kernel, seqs, heads), out_shape=sh...  61.8 us
    pallas_call x1, Pallas kernels, fused_shards(): pl.pallas_call(write_kernel, out_shape=shapes, in_specs=[hbm] * 5, out_sp...  3.85 us

profile of v5, /device:TPU:0, one launch (start us, length us, event | category | flops | bytes accessed | tf_op | source)
XLA Modules:
  0.0 66.3 jit_solution(15760902180536669841)
XLA Ops:
  0.6 61.8 %layer.1 = (bf16[1,2,256,512]{3,2,1,0:T(8,128)(2,1)}, f32[512,256]{1,0:T(8,128)}, f32[1,2,256,512]{3,2,1,0:T(8,128)}, f32[1,2,256,512]{3,2,1,0:T(8,128)}, f32[1,2,512,256]{3,2,1,0:T(8,128)}) custom-call(bf16[1,2,256,512]{3,2,1,0:T(8,128)(2,1)} %q_ref.1, bf16[1,2,256,512]{3,2,1,0:T(8,128)(2,1)} %k_ref.1, bf16[1,2,256,512]{3,2,1,0:T(8,128)(2,1)} %v_ref.1, ...), custom_call_target="tpu_custom_call" | custom-call | flops 5000000000 | bytes 10485760 | tf_op jit(solution)/shard_map/layer/pallas_call | solution.py:763
  62.5 3.9 %write.1 = (bf16[1,2,256,512]{3,2,1,0:T(8,128)(2,1)}, f32[512,256]{1,0:T(8,128)}, f32[1,2,256,512]{3,2,1,0:T(8,128)}, f32[1,2,256,512]{3,2,1,0:T(8,128)}, f32[1,2,512,256]{3,2,1,0:T(8,128)}) custom-call(bf16[1,2,256,512]{3,2,1,0:T(8,128)(2,1)} %get-tuple-element.10.refs_0_, f32[512,256]{1,0:T(8,128)} %get-tuple-element.11.refs_1_, ...), custom_call_target="tpu_custom_call" | custom-call | tf_op jit(solution)/shard_map/write/pallas_call | solution.py:838

commit v6 on v4

--- a/solution.py
+++ b/solution.py
@@ -677,12 +677,13 @@
         grad_step(t)
     release(1)
     forward(1)
+    for b in range(blocks - 1):
+        finish(b)
     if last > 1:
         gather_step(last, 0)
         gather_step(last, 1)
         grad_step(last)
-    for b in range(blocks):
-        finish(b)
+    finish(blocks - 1)
     for copy in finals:
         copy.wait()
     for s2 in range(seqs):

time: 66.3 us -> 66.3 us (level)
  no operation moved by 1% of the time
where the time goes in v6:
time: 66.3 us; the launch traced here: 66.1 us
  Pallas kernels  65.5 us (99%)
    pallas_call x1, Pallas kernels, fused_shards(): pl.pallas_call(functools.partial(layer_kernel, seqs, heads), out_shape=sh...  61.6 us
    pallas_call x1, Pallas kernels, fused_shards(): pl.pallas_call(write_kernel, out_shape=shapes, in_specs=[hbm] * 5, out_sp...  3.85 us

profile of v6, /device:TPU:0, one launch (start us, length us, event | category | flops | bytes accessed | tf_op | source)
XLA Modules:
  0.0 66.1 jit_solution(2160523397900973275)
XLA Ops:
  0.6 61.6 %layer.1 = (bf16[1,2,256,512]{3,2,1,0:T(8,128)(2,1)}, f32[512,256]{1,0:T(8,128)}, f32[1,2,256,512]{3,2,1,0:T(8,128)}, f32[1,2,256,512]{3,2,1,0:T(8,128)}, f32[1,2,512,256]{3,2,1,0:T(8,128)}) custom-call(bf16[1,2,256,512]{3,2,1,0:T(8,128)(2,1)} %q_ref.1, bf16[1,2,256,512]{3,2,1,0:T(8,128)(2,1)} %k_ref.1, bf16[1,2,256,512]{3,2,1,0:T(8,128)(2,1)} %v_ref.1, ...), custom_call_target="tpu_custom_call" | custom-call | flops 5000000000 | bytes 10485760 | tf_op jit(solution)/shard_map/layer/pallas_call | solution.py:765
  62.3 3.9 %write.1 = (bf16[1,2,256,512]{3,2,1,0:T(8,128)(2,1)}, f32[512,256]{1,0:T(8,128)}, f32[1,2,256,512]{3,2,1,0:T(8,128)}, f32[1,2,256,512]{3,2,1,0:T(8,128)}, f32[1,2,512,256]{3,2,1,0:T(8,128)}) custom-call(bf16[1,2,256,512]{3,2,1,0:T(8,128)(2,1)} %get-tuple-element.10.refs_0_, f32[512,256]{1,0:T(8,128)} %get-tuple-element.11.refs_1_, ...), custom_call_target="tpu_custom_call" | custom-call | tf_op jit(solution)/shard_map/write/pallas_call | solution.py:840
